TPU v7x, 32 devices: a whole 2x2x4 slice. The times are simulated.
32 devices in a mesh: blk: 16 (over z, x, core), group: 2 (over y).
Axes of the slice: x: 2, y: 2, z: 4, core: 2. Of those that a mesh axis runs over, the one named last changes fastest.
Arguments:
- user_factors: float32 [2, 16384, 256], P('group', 'blk'), may hold values from -1.5 to 1.5
- item_factors: float32 [2, 4096, 256], P('group', 'blk'), may hold values from -1.5 to 1.5
- ratings: bfloat16 [2, 16, 2, 2, 256, 256], P('group', 'blk'), may hold values from -6 to 6
- tile_rows: int32 [2, 16, 2, 2], P('group', 'blk'), may hold values from 0 to 3, as said below
- counts: int32 [2, 16, 2], P('group', 'blk'), may hold values from 0 to 2
- plan: int32 [2, 16], replicated, may hold values from 0 to 15, as said below
Outputs:
- user_out: float32 [2, 16384, 256], P('group', 'blk')
- received: bfloat16 [2, 16, 4, 256, 256], P('group', 'blk')
Inputs may be any that keep to these rules, and one draw needn't show every extreme that they name: `tile_rows`: within one stop of one device the 2 entries differ. `plan`: in every group no device receives more than 4 blocks, and some device receives exactly 4.
All inputs are finite; a program needn't handle non-finite values.
Results may differ from a plain program's by a relative error of at most 0.006.
Values may be sent and summed in bfloat16 or wider, within the bound.
A program may use at most 64 MiB of HBM per device.

v0:
```python
import jax
import jax.numpy as jnp
from jax import lax
from jax.sharding import PartitionSpec as P

CAP = 4


learn_rate = 0.01
shrinkage = 0.05


def shifted_2(block, axis, distance):
    devices = range(lax.axis_size(axis))
    route = [((i - distance) % len(devices), i) for i in devices]
    return lax.ppermute(block, axis, route)


def stop_update(user_rows, item_block, rating_tiles, row_ids, tile_count):
    tile_size = rating_tiles.shape[1]
    item_low = item_block.astype(jnp.bfloat16)
    grad_items = jnp.zeros(item_block.shape, jnp.float32)
    for slot_index in range(rating_tiles.shape[0]):
        active = (slot_index < tile_count).astype(jnp.float32)
        first_row = row_ids[slot_index] * tile_size
        before = lax.dynamic_slice_in_dim(user_rows, first_row, tile_size, 0)
        user_low = before.astype(jnp.bfloat16)
        predicted = lax.dot_general(
            user_low, item_low, (((1,), (1,)), ((), ())), preferred_element_type=jnp.float32
        )
        residual = (active * (rating_tiles[slot_index].astype(jnp.float32) - predicted)).astype(
            jnp.bfloat16
        )
        user_step = jnp.dot(residual, item_low, preferred_element_type=jnp.float32)
        grad_items = grad_items + lax.dot_general(
            residual, user_low, (((0,), (0,)), ((), ())), preferred_element_type=jnp.float32
        )
        change = learn_rate * active * (user_step - shrinkage * before)
        user_rows = lax.dynamic_update_slice_in_dim(user_rows, before + change, first_row, 0)
    item_block = item_block + learn_rate * (
        grad_items - shrinkage * tile_count.astype(jnp.float32) * item_block
    )
    return (user_rows, item_block)


def shards(user_factors, item_factors, ratings, tile_rows, counts, plan):
    user_rows = user_factors[0]
    item_block = item_factors[0]
    rating_tiles = ratings[0, 0]
    row_table = tile_rows[0, 0]
    count_table = counts[0, 0]
    stop_count = rating_tiles.shape[0]
    user_rows, item_block = stop_update(
        user_rows, item_block, rating_tiles[0], row_table[0], count_table[0]
    )

    def advance(stop_index, carried):
        rows_now, block_now = carried
        block_now = shifted_2(block_now, "blk", 1)
        return stop_update(
            rows_now,
            block_now,
            rating_tiles[stop_index],
            row_table[stop_index],
            count_table[stop_index],
        )

    user_rows, item_block = lax.fori_loop(1, stop_count, advance, (user_rows, item_block))
    handed = item_block.astype(jnp.bfloat16)
    shifted = shifted_2(handed, "group", 1)
    blocks = lax.axis_size("blk")
    groups = lax.axis_size("group")
    source_group = (lax.axis_index("group") + groups - 1) % groups
    group_pick = jnp.arange(groups) == source_group
    plan_row = jnp.sum(jnp.where(group_pick[:, None], plan, 0), axis=0)
    positions = jnp.arange(blocks)
    earlier = positions[None, :] < positions[:, None]
    slot_of = jnp.sum(
        ((plan_row[:, None] == plan_row[None, :]) & earlier).astype(jnp.int32), axis=1
    )
    held_block = (positions - stop_count + 1 + blocks) % blocks
    block_pick = held_block[:, None] == positions[None, :]
    dest_at = jnp.sum(jnp.where(block_pick, plan_row[None, :], 0), axis=1)
    slot_at = jnp.sum(jnp.where(block_pick, slot_of[None, :], 0), axis=1)
    slot_ids = jnp.arange(CAP)
    piece_width = shifted.size // blocks
    pieces_out = shifted.reshape(blocks, piece_width)
    pieces_in = lax.all_to_all(pieces_out, "blk", split_axis=0, concat_axis=0, tiled=True)
    selector = (
        (dest_at[None, None, :] == positions[None, :, None])
        & (slot_at[None, None, :] == slot_ids[:, None, None])
    ).astype(jnp.bfloat16)
    outbound = jnp.einsum(
        "cdp,pw->cdw", selector, pieces_in, preferred_element_type=jnp.float32
    ).astype(jnp.bfloat16)
    arrived = lax.all_to_all(outbound, "blk", split_axis=1, concat_axis=1, tiled=True)
    gathered = arrived.reshape(CAP, -1)
    received = gathered.reshape(1, 1, CAP, item_block.shape[0], item_block.shape[1])
    return (user_rows[None], received)


def solution(mesh):
    in_specs = (
        P("group", "blk", None),
        P("group", "blk", None),
        P("group", "blk", None, None, None, None),
        P("group", "blk", None, None),
        P("group", "blk", None),
        P(),
    )
    out_specs = (P("group", "blk", None), P("group", "blk", None, None, None))
    return jax.shard_map(shards, mesh=mesh, in_specs=in_specs, out_specs=out_specs, check_vma=False)
```

profile of v0, /device:TPU:0, one launch (start us, length us, event | category | flops | bytes accessed | tf_op | source)
XLA Modules:
  0.0 61.5 jit_solution(16205237208813479878)
XLA Ops:
  0.6 0.0 copy-start.1
  0.6 1.4 %fusion.48 = (s32[1,1,1,1]{3,2,1,0:T(1,128)}, s32[1,1,1,1]{3,2,1,0:T(1,128)}, s32[1,1,1,1]{3,2,1,0:T(1,128)}, s32[1,1,1,1]{3,2,1,0:T(1,128)}) fusion(s32[1,1,2,2]{3,2,1,0:T(2,128)} %param.9), kind=kLoop, calls=%fused_computation.76 | loop fusion | bytes 32 | tf_op jit(solution)/shard_map/while/body/eval_jaxpr/slice | solution.py:25
  3.3 1.3 %fusion.49 = (s32[1,1,1]{2,1,0:T(1,128)}, s32[1,1,1]{2,1,0:T(1,128)}) fusion(s32[1,1,2]{2,1,0:T(1,128)} %param.10), kind=kLoop, calls=%fused_computation.77 | loop fusion | bytes 16 | tf_op jit(solution)/shard_map/while/body/eval_jaxpr/dynamic_slice | solution.py:65
  6.4 1.3 %fusion.20 = bf16[256,256]{1,0:T(8,128)(2,1)S(1)} fusion(f32[1,1024,256]{2,1,0:T(8,128)} %param.6, s32[]{:T(128)S(6)} %select_n.52, f32[1,256,256]{2,1,0:T(8,128)} %param.7, bf16[1,1,2,2,256,256]{5,4,3,2,1,0:T(8,128)(2,1)} %param.8, f32[]{:T(128)} %bitcast.4), kind=kOutput, calls=%fused_computation.31 | convolution fusion | flops 33882112 | bytes 655876 | tf_op jit(solution)/shard_map/dot_general | solution.py:28
  7.7 1.2 %fusion.26 = f32[256,256]{1,0:T(8,128)S(1)} fusion(bf16[256,256]{1,0:T(8,128)(2,1)S(1)} %fusion.20, f32[1,1024,256]{2,1,0:T(8,128)} %param.6, s32[]{:T(128)S(6)} %select_n.52), kind=kOutput, calls=%fused_computation.45 | convolution fusion | flops 33554432 | bytes 524292 | tf_op jit(solution)/shard_map/dot_general | solution.py:35
  8.9 0.0 copy-done.1
  8.9 0.0 copy-start
  8.9 0.1 copy.21
  9.0 0.0 copy-start.3
  9.0 0.8 %copy-done = f32[1,256,256]{2,1,0:T(8,128)S(1)} copy-done((f32[1,256,256]{2,1,0:T(8,128)S(1)}, f32[1,256,256]{2,1,0:T(8,128)}, u32[]{:S(2)}) %copy-start) | copy-done | bytes 262168
  9.9 0.2 fusion.17
  10.1 0.0 copy-done.3
  10.1 0.2 fusion.21
  10.3 0.2 fusion.19
  10.6 0.5 collective-permute-start
  11.1 0.0 copy-start.4
  11.1 0.7 %copy-done.4 = s32[2,16]{1,0:T(2,128)S(1)} copy-done((s32[2,16]{1,0:T(2,128)S(1)}, s32[2,16]{1,0:T(2,128)}, u32[]{:S(2)}) %copy-start.4) | copy-done | bytes 152
  11.7 0.1 select_reduce_fusion.2
  11.8 0.2 convert_reduce_fusion
  15.3 0.2 fusion.13
  15.5 4.6 %collective-permute-done = f32[256,256]{1,0:T(8,128)S(1)} collective-permute-done((f32[256,256]{1,0:T(8,128)S(1)}, f32[256,256]{1,0:T(8,128)S(1)}, u32[]{:S(2)}, u32[]{:S(2)}) %collective-permute-start) | collective-permute-done | bytes 262176 | tf_op jit(solution)/shard_map/while/body/eval_jaxpr/ppermute | solution.py:16
  20.1 0.2 fusion.22
  20.3 0.2 fusion.31
  20.6 0.2 fusion.7
  20.8 0.2 fusion.23
  21.0 0.2 add_convert_fusion
  21.2 2.1 %collective-permute-start.1 = (bf16[256,256]{1,0:T(8,128)(2,1)S(1)}, bf16[256,256]{1,0:T(8,128)(2,1)S(1)}, u32[]{:S(2)}, u32[]{:S(2)}) collective-permute-start(bf16[256,256]{1,0:T(8,128)(2,1)S(1)} %add_convert_fusion), channel_id=1, source_target_pairs={{1,0},{0,1},{3,2},{2,3},{5,4},{4,5},{7,6},{6,7},{9,8},{8,9},{11,10... | collective-permute-start | bytes 393224 | tf_op jit(solution)/shard_map/ppermute | solution.py:16
  23.3 0.2 select_reduce_fusion.1
  23.5 2.8 %collective-permute-done.1 = bf16[256,256]{1,0:T(8,128)(2,1)S(1)} collective-permute-done((bf16[256,256]{1,0:T(8,128)(2,1)S(1)}, bf16[256,256]{1,0:T(8,128)(2,1)S(1)}, u32[]{:S(2)}, u32[]{:S(2)}) %collective-permute-start.1) | collective-permute-done | bytes 131104 | tf_op jit(solution)/shard_map/ppermute | solution.py:16
  26.3 0.5 broadcast.99
  26.8 1.4 %reduce = bf16[16,4096]{1,0:T(8,128)(2,1)S(1)} reduce(bf16[16,1,4096]{2,1,0:T(2,128)(2,1)S(1)} %all_to_all.15, bf16[]{:T(256)} %broadcast.99), dimensions={1}, to_apply=%all_to_all.15.reduce_sub_computation | reduce | bytes 262146 | tf_op jit(solution)/shard_map/all_to_all | solution.py:88
  28.2 0.7 %reshape.169 = bf16[16,2,2048]{2,1,0:T(2,128)(2,1)} reshape(bf16[16,4096]{1,0:T(8,128)(2,1)S(1)} %reduce) | data formatting | bytes 262144
  29.0 3.7 %all-to-all-start = ((bf16[16,2,2048]{2,1,0:T(2,128)(2,1)}), bf16[16,2,2048]{2,1,0:T(2,128)(2,1)S(1)}, u32[]{:S(2)}, u32[]{:S(2)}) async-start(bf16[16,2,2048]{2,1,0:T(2,128)(2,1)} %reshape.169), calls=%async_computation | async-start | bytes 262144 | tf_op jit(solution)/shard_map/all_to_all | solution.py:88
  32.7 7.9 %all-to-all-done = bf16[16,2,2048]{2,1,0:T(2,128)(2,1)S(1)} async-done(((bf16[16,2,2048]{2,1,0:T(2,128)(2,1)}), bf16[16,2,2048]{2,1,0:T(2,128)(2,1)S(1)}, u32[]{:S(2)}, u32[]{:S(2)}) %all-to-all-start) | async-done | bytes 131104 | tf_op jit(solution)/shard_map/all_to_all | solution.py:88
  40.6 0.1 reshape.170
  40.7 0.3 convolution_convert_fusion
  41.0 1.2 %copy.14 = bf16[4,16,4096]{2,0,1:T(4,128)(2,1)} copy(bf16[4,16,4096]{2,1,0:T(8,128)(2,1)S(1)} %convolution_convert_fusion) | data formatting | bytes 1048576 | tf_op jit(solution)/shard_map/convert_element_type | solution.py:95
  42.2 3.6 %all-to-all-start.1 = ((bf16[4,16,4096]{2,0,1:T(4,128)(2,1)}), bf16[4,16,4096]{2,0,1:T(4,128)(2,1)S(1)}, u32[]{:S(2)}, u32[]{:S(2)}) async-start(bf16[4,16,4096]{2,0,1:T(4,128)(2,1)} %copy.14), calls=%async_computation.1 | async-start | bytes 1048576 | tf_op jit(solution)/shard_map/all_to_all | solution.py:96
  45.8 0.1 copy.24
  45.9 0.2 fusion.3
  46.1 0.0 copy-start.2
  46.1 14.1 %all-to-all-done.1 = bf16[4,16,4096]{2,0,1:T(4,128)(2,1)S(1)} async-done(((bf16[4,16,4096]{2,0,1:T(4,128)(2,1)}), bf16[4,16,4096]{2,0,1:T(4,128)(2,1)S(1)}, u32[]{:S(2)}, u32[]{:S(2)}) %all-to-all-start.1) | async-done | bytes 524320 | tf_op jit(solution)/shard_map/all_to_all | solution.py:96
  60.2 0.3 copy.15
  60.5 1.0 %reshape_reshape.3 = bf16[1,1,4,256,256]{4,3,2,1,0:T(8,128)(2,1)} reshape(bf16[4,16,4096]{2,1,0:T(8,128)(2,1)S(1)} %copy.15) | data formatting | bytes 1048576 | tf_op jit(solution)/shard_map/reshape;reshape | solution.py:98
  61.5 0.0 copy-done.2
  (6 shorter events, 0.1 us)
Async XLA Ops:
  0.6 8.3 %copy-start.1 = (f32[1,1024,256]{2,1,0:T(8,128)S(1)}, f32[1,1024,256]{2,1,0:T(8,128)}, u32[]{:S(2)}) copy-start(f32[1,1024,256]{2,1,0:T(8,128)} %param.6) | copy-start | bytes 3145732
  8.9 1.0 %copy-start = (f32[1,256,256]{2,1,0:T(8,128)S(1)}, f32[1,256,256]{2,1,0:T(8,128)}, u32[]{:S(2)}) copy-start(f32[1,256,256]{2,1,0:T(8,128)} %param.7) | copy-start | bytes 786436
  9.0 1.1 %copy-start.3 = (bf16[1,1,2,2,256,256]{5,4,3,2,1,0:T(8,128)(2,1)S(1)}, bf16[1,1,2,2,256,256]{5,4,3,2,1,0:T(8,128)(2,1)}, u32[]{:S(2)}) copy-start(bf16[1,1,2,2,256,256]{5,4,3,2,1,0:T(8,128)(2,1)} %param.8) | copy-start | bytes 1572868
  10.6 9.5 %collective-permute-start = (f32[256,256]{1,0:T(8,128)S(1)}, f32[256,256]{1,0:T(8,128)S(1)}, u32[]{:S(2)}, u32[]{:S(2)}) collective-permute-start(f32[256,256]{1,0:T(8,128)S(1)} %fusion.19), channel_id=1, source_target_pairs={{30,0},{0,2},{2,4},{4,6},{6,8},{8,10},{10,12},{12,14},{14,16},{16,... | collective-permute-start | bytes 786440 | tf_op jit(solution)/shard_map/while/body/eval_jaxpr/ppermute | solution.py:16
  11.1 0.7 %copy-start.4 = (s32[2,16]{1,0:T(2,128)S(1)}, s32[2,16]{1,0:T(2,128)}, u32[]{:S(2)}) copy-start(s32[2,16]{1,0:T(2,128)} %param.11) | copy-start | bytes 388
  21.2 5.0 %collective-permute-start.1 = (bf16[256,256]{1,0:T(8,128)(2,1)S(1)}, bf16[256,256]{1,0:T(8,128)(2,1)S(1)}, u32[]{:S(2)}, u32[]{:S(2)}) collective-permute-start(bf16[256,256]{1,0:T(8,128)(2,1)S(1)} %add_convert_fusion), channel_id=1, source_target_pairs={{1,0},{0,1},{3,2},{2,3},{5,4},{4,5},{7,6},{6,7},{9,8},{8,9},{11,10... | collective-permute-start | bytes 393224 | tf_op jit(solution)/shard_map/ppermute | solution.py:16
  29.0 11.6 %all-to-all-start = ((bf16[16,2,2048]{2,1,0:T(2,128)(2,1)}), bf16[16,2,2048]{2,1,0:T(2,128)(2,1)S(1)}, u32[]{:S(2)}, u32[]{:S(2)}) async-start(bf16[16,2,2048]{2,1,0:T(2,128)(2,1)} %reshape.169), calls=%async_computation | async-start | bytes 262144 | tf_op jit(solution)/shard_map/all_to_all | solution.py:88
  42.2 18.0 %all-to-all-start.1 = ((bf16[4,16,4096]{2,0,1:T(4,128)(2,1)}), bf16[4,16,4096]{2,0,1:T(4,128)(2,1)S(1)}, u32[]{:S(2)}, u32[]{:S(2)}) async-start(bf16[4,16,4096]{2,0,1:T(4,128)(2,1)} %copy.14), calls=%async_computation.1 | async-start | bytes 1048576 | tf_op jit(solution)/shard_map/all_to_all | solution.py:96
  46.1 15.5 %copy-start.2 = (f32[1,1024,256]{2,1,0:T(8,128)}, f32[1,1024,256]{2,1,0:T(8,128)S(1)}, u32[]{:S(2)}) copy-start(f32[1,1024,256]{2,1,0:T(8,128)S(1)} %fusion.3) | copy-start | bytes 3145732
where the time goes:
time: 62.1 us; the launch traced here: 61.5 us
  waiting for transfers between devices  29.4 us (47%)
  starting transfers between devices  9.81 us (16%)
  local copies, waits for them, and re-layouts  8.35 us (13%)
  between operations  7.24 us (12%)
  matrix products  4.9 us (8%)
  other arithmetic  1.87 us (3%)
    all_to_all x1, waiting for transfers between devices, shards(): lax.all_to_all(outbound, 'blk', split_axis=1, concat_axis=1, tiled=True)  14.1 us
    all_to_all x1, waiting for transfers between devices, shards(): lax.all_to_all(pieces_out, 'blk', split_axis=0, concat_axis=0, tiled=True)  7.91 us
    ppermute x2, waiting for transfers between devices, shifted_2(): return lax.ppermute(block, axis, route)  7.35 us
    all_to_all x1, starting transfers between devices, shards(): lax.all_to_all(pieces_out, 'blk', split_axis=0, concat_axis=0, tiled=True)  3.68 us
    all_to_all x1, starting transfers between devices, shards(): lax.all_to_all(outbound, 'blk', split_axis=1, concat_axis=1, tiled=True)  3.57 us
    ppermute x2, starting transfers between devices, shifted_2(): return lax.ppermute(block, axis, route)  2.56 us
    unnamed x14, local copies, waits for them, and re-layouts  2.52 us
    dot_general x4, matrix products, stop_update(): lax.dot_general(user_low, item_low, (((1,), (1,)), ((), ())), preferred_e...  1.97 us
  transfers between devices with their start and end apart: 4, of which 4 were waited for; matrix products, arithmetic and copies ran while one was open for 2% of the time, Pallas kernels for 0%

commit v1 on v0

v1 whole, which is shorter than its diff:
```python
import functools

import jax
import jax.numpy as jnp
from jax import lax
from jax.experimental import pallas as pl
from jax.experimental.pallas import tpu as pltpu
from jax.sharding import PartitionSpec as P

CAP = 4
PARTS = 2

learn_rate = 0.01
shrinkage = 0.05

MESH = pl.DeviceIdType.MESH
F32 = jnp.float32
LOW = jnp.bfloat16


def kernel(
    blocks, groups, parts,
    users, items, ratings, row_table, count_table, plan,
    users_out, received,
    ring_out, ring_in, handed, gathered, staged, change, picks,
    ring_send, ring_recv, part_send, part_recv, slot_send, slot_recv, own_sem,
):
    stops, capt = ratings.shape[0], ratings.shape[1]
    tiles = users.shape[0]
    lanes = blocks // parts
    depth = gathered.shape[1]
    me = lax.axis_index("blk")
    group = lax.axis_index("group")
    ahead, behind = lax.rem(group + 1, groups), lax.rem(group + groups - 1, groups)
    right, left = lax.rem(me + 1, blocks), lax.rem(me + blocks - 1, blocks)
    part_first = (me // lanes) * lanes
    lane = me - part_first

    barrier = pltpu.get_barrier_semaphore()
    pl.semaphore_signal(barrier, inc=1, device_id=(left, group), device_id_type=MESH)
    for step in range(blocks):
        pl.semaphore_signal(
            barrier, inc=1, device_id=(lax.rem(me + step, blocks), behind), device_id_type=MESH
        )
    for step in range(1, lanes):
        other = part_first + lax.rem(lane + step, lanes)
        pl.semaphore_signal(barrier, inc=1, device_id=(other, group), device_id_type=MESH)

    change[capt] = jnp.zeros(change.shape[1:], F32)
    gathered[blocks] = jnp.zeros(gathered.shape[1:], LOW)

    def ring_copy(stop, half):
        return pltpu.make_async_remote_copy(
            src_ref=ring_out.at[stop, half],
            dst_ref=ring_in.at[stop, half],
            send_sem=ring_send.at[stop, half],
            recv_sem=ring_recv.at[stop, half],
            device_id=(right, group),
            device_id_type=MESH,
        )

    def part_copy(step):
        target = lax.rem(me + step, blocks)
        first = pl.multiple_of(lax.rem(target, lanes) * depth, depth)
        return pltpu.make_async_remote_copy(
            src_ref=handed.at[pl.ds(first, depth)],
            dst_ref=gathered.at[me],
            send_sem=part_send.at[step],
            recv_sem=part_recv.at[me],
            device_id=(target, ahead),
            device_id_type=MESH,
        )

    rows_here = pl.ds(pl.multiple_of(lane * depth, depth), depth)

    def slot_copy(step):
        return pltpu.make_async_remote_copy(
            src_ref=staged.at[step],
            dst_ref=received.at[:, rows_here],
            send_sem=slot_send.at[step],
            recv_sem=slot_recv.at[lane],
            device_id=(part_first + lax.rem(lane + step, lanes), group),
            device_id_type=MESH,
        )

    for stop in range(stops):
        source = users if stop == 0 else users_out
        count = count_table[stop]
        if stop == 0:
            item_low = items[...].astype(LOW)
        else:
            ring_copy(stop - 1, 0).wait_recv()
            item_low = ring_in[stop - 1, 0]
        grad = jnp.zeros(items.shape, F32)
        kept = []
        for c in range(capt):
            active = (c < count).astype(F32)
            before = source[row_table[stop, c]]
            user_low = before.astype(LOW)
            predicted = lax.dot_general(
                user_low, item_low, (((1,), (1,)), ((), ())), preferred_element_type=F32
            )
            residual = (active * (ratings[stop, c].astype(F32) - predicted)).astype(LOW)
            grad = grad + lax.dot_general(
                residual, user_low, (((0,), (0,)), ((), ())), preferred_element_type=F32
            )
            kept.append((active, residual))
        if stop == 0:
            block = items[...]
        else:
            ring_copy(stop - 1, 1).wait_recv()
            block = ring_in[stop - 1, 0].astype(F32) + ring_in[stop - 1, 1].astype(F32)
        block = block + learn_rate * (grad - shrinkage * count.astype(F32) * block)
        if stop == 0:
            pl.semaphore_wait(barrier, blocks + lanes)
        if stop < stops - 1:
            high = block.astype(LOW)
            ring_out[stop, 0] = high
            ring_copy(stop, 0).start()
            ring_out[stop, 1] = (block - high.astype(F32)).astype(LOW)
            ring_copy(stop, 1).start()
        else:
            handed[...] = block.astype(LOW)
            for step in range(blocks):
                part_copy(step).start()
        for c in range(capt):
            active, residual = kept[c]
            before = source[row_table[stop, c]]
            user_step = jnp.dot(residual, item_low, preferred_element_type=F32)
            change[c] = learn_rate * active * (user_step - shrinkage * before)
        for tile in range(tiles):
            which = jnp.int32(capt)
            for c in range(capt):
                which = jnp.where(row_table[stop, c] == tile, c, which)
            users_out[tile] = source[tile] + change[which]

    def find(step, carry):
        target = part_first + lax.rem(lane + step, lanes)
        seen = jnp.int32(0)
        found = [jnp.int32(blocks)] * CAP
        for k in range(blocks):
            match = plan[behind, k] == target
            for c in range(CAP):
                found[c] = jnp.where(match & (seen == c), k, found[c])
            seen = seen + match.astype(jnp.int32)
        for c in range(CAP):
            picks[step, c] = found[c]
        return carry

    lax.fori_loop(0, lanes, find, 0)

    for k in range(blocks):
        pltpu.make_async_remote_copy(
            src_ref=gathered.at[k],
            dst_ref=gathered.at[k],
            send_sem=part_send.at[k],
            recv_sem=part_recv.at[k],
            device_id=(k, behind),
            device_id_type=MESH,
        ).wait_recv()

    def held_by(k):
        place = lax.rem(k + (stops - 1), blocks)
        return jnp.where(k == blocks, blocks, place)

    for step in list(range(1, lanes)) + [0]:
        for c in range(CAP):
            staged[step, c] = gathered[held_by(picks[step, c])]
        if step > 0:
            slot_copy(step).start()
    own = pltpu.make_async_copy(staged.at[0], received.at[:, rows_here], own_sem)
    own.start()
    own.wait()
    for step in range(1, lanes):
        sender = lax.rem(lane + step, lanes)
        rows = pl.ds(pl.multiple_of(sender * depth, depth), depth)
        pltpu.make_async_remote_copy(
            src_ref=staged.at[step],
            dst_ref=received.at[:, rows],
            send_sem=slot_send.at[step],
            recv_sem=slot_recv.at[sender],
            device_id=(part_first + sender, group),
            device_id_type=MESH,
        ).wait_recv()
    for step in range(1, lanes):
        slot_copy(step).wait_send()
    for step in range(blocks):
        part_copy(step).wait_send()
    for stop in range(stops - 1):
        for half in range(2):
            ring_copy(stop, half).wait_send()


def shards(user_factors, item_factors, ratings, tile_rows, counts, plan):
    blocks, groups = lax.axis_size("blk"), lax.axis_size("group")
    _, _, stops, capt, tile, _ = ratings.shape
    _, rows, rank = user_factors.shape
    depth_all = item_factors.shape[1]
    parts = max(PARTS, blocks * 16 // depth_all)
    lanes = blocks // parts
    depth = depth_all // lanes
    vmem = pl.BlockSpec(memory_space=pltpu.VMEM)
    smem = pl.BlockSpec(memory_space=pltpu.SMEM)
    hops = max(stops - 1, 1)
    users, received = pl.pallas_call(
        functools.partial(kernel, blocks, groups, parts),
        out_shape=(
            jax.ShapeDtypeStruct((rows // tile, tile, rank), F32),
            jax.ShapeDtypeStruct((CAP, depth_all, rank), LOW),
        ),
        in_specs=[vmem, vmem, vmem, smem, smem, smem],
        out_specs=(vmem, vmem),
        scratch_shapes=[
            pltpu.VMEM((hops, 2, depth_all, rank), LOW),
            pltpu.VMEM((hops, 2, depth_all, rank), LOW),
            pltpu.VMEM((depth_all, rank), LOW),
            pltpu.VMEM((blocks + 1, depth, rank), LOW),
            pltpu.VMEM((lanes, CAP, depth, rank), LOW),
            pltpu.VMEM((capt + 1, tile, rank), F32),
            pltpu.SMEM((lanes, CAP), jnp.int32),
            pltpu.SemaphoreType.DMA((hops, 2)),
            pltpu.SemaphoreType.DMA((hops, 2)),
            pltpu.SemaphoreType.DMA((blocks,)),
            pltpu.SemaphoreType.DMA((blocks,)),
            pltpu.SemaphoreType.DMA((lanes,)),
            pltpu.SemaphoreType.DMA((lanes,)),
            pltpu.SemaphoreType.DMA,
        ],
        compiler_params=pltpu.CompilerParams(
            collective_id=0, has_side_effects=True, vmem_limit_bytes=48 * 1024 * 1024
        ),
        cost_estimate=pl.CostEstimate(
            flops=6 * stops * capt * tile * depth_all * rank,
            bytes_accessed=2 * rows * rank * 4,
            transcendentals=0,
        ),
    )(
        user_factors.reshape(rows // tile, tile, rank),
        item_factors[0],
        ratings[0, 0],
        tile_rows[0, 0],
        counts[0, 0],
        plan,
    )
    return users.reshape(1, rows, rank), received[None, None]


def solution(mesh):
    in_specs = (
        P("group", "blk", None),
        P("group", "blk", None),
        P("group", "blk", None, None, None, None),
        P("group", "blk", None, None),
        P("group", "blk", None),
        P(),
    )
    out_specs = (P("group", "blk", None), P("group", "blk", None, None, None))
    return jax.shard_map(shards, mesh=mesh, in_specs=in_specs, out_specs=out_specs, check_vma=False)
```

time: 62.1 us -> 31.8 us (0.51)
  waiting for transfers between devices: 29.4 us -> 0 us
  Pallas kernels: 0 us -> 25 us
  starting transfers between devices: 9.81 us -> 0 us
  between operations: 7.24 us -> 0.67 us
  matrix products: 4.9 us -> 0 us
  local copies, waits for them, and re-layouts: 8.35 us -> 5.65 us
  other arithmetic: 1.87 us -> 0 us
    pallas_call x0 -> x1, Pallas kernels: none -> 25 us  [shards(): pl.pallas_call(functools.partial(kernel, blocks, groups, parts), out_shap...]
    all_to_all x2 -> x0, waiting for transfers between devices: 22 us -> none  [the longest x1 14.1 us: shards(): lax.all_to_all(outbound, 'blk', split_axis=1, concat_axis=1, tiled=True)]
    ppermute x2 -> x0, waiting for transfers between devices: 7.35 us -> none  [shifted_2(): return lax.ppermute(block, axis, route)]
    all_to_all x2 -> x0, starting transfers between devices: 7.25 us -> none  [the longest x1 3.68 us: shards(): lax.all_to_all(pieces_out, 'blk', split_axis=0, concat_axis=0, tiled=True)]
    dot_general x13 -> x0, matrix products: 4.9 us -> none  [the longest x4 1.97 us: stop_update(): lax.dot_general(user_low, item_low, (((1,), (1,)), ((), ())), preferred_e...]
    unnamed x14, local copies, waits for them, and re-layouts: 2.52 us -> 5.65 us
    ppermute x2 -> x0, starting transfers between devices: 2.56 us -> none  [shifted_2(): return lax.ppermute(block, axis, route)]
    slice x1 -> x0, local copies, waits for them, and re-layouts: 1.42 us -> none  [stop_update(): first_row = row_ids[slot_index] * tile_size]
  transfers between devices with their start and end apart: 4 -> 0, of which waited for: 4 -> 0; matrix products, arithmetic and copies ran while one was open for 2% -> 0% of each run, Pallas kernels for 0% -> 0%
where the time goes in v1:
time: 31.8 us; the launch traced here: 31.3 us
  Pallas kernels  25 us (79%)
  local copies, waits for them, and re-layouts  5.65 us (18%)
  between operations  0.67 us (2%)
    pallas_call x1, Pallas kernels, shards(): pl.pallas_call(functools.partial(kernel, blocks, groups, parts), out_shap...  25 us
    unnamed x14, local copies, waits for them, and re-layouts  5.65 us

profile of v1, /device:TPU:0, one launch (start us, length us, event | category | flops | bytes accessed | tf_op | source)
XLA Modules:
  0.0 31.3 jit_solution(6717301439021478295)
XLA Ops:
  0.6 0.0 copy-start.4
  0.6 0.0 copy-start.3
  0.7 0.0 copy-start.5
  0.7 0.7 %copy-done.4 = s32[2,16]{1,0:T(2,128)S(1)} copy-done((s32[2,16]{1,0:T(2,128)S(1)}, s32[2,16]{1,0:T(2,128)}, u32[]{:S(2)}) %copy-start.4) | copy-done | bytes 152
  1.3 0.0 copy-done.3
  1.3 0.0 copy-done.5
  1.3 0.0 copy-start
  1.3 1.2 %copy-done = f32[1,1024,256]{2,1,0:T(8,128)S(1)} copy-done((f32[1,1024,256]{2,1,0:T(8,128)S(1)}, f32[1,1024,256]{2,1,0:T(8,128)}, u32[]{:S(2)}) %copy-start) | copy-done | bytes 1048600
  2.6 0.0 copy-start.1
  2.6 1.0 %copy-done.1 = bf16[1,1,2,2,256,256]{5,4,3,2,1,0:T(8,128)(2,1)S(1)} copy-done((bf16[1,1,2,2,256,256]{5,4,3,2,1,0:T(8,128)(2,1)S(1)}, bf16[1,1,2,2,256,256]{5,4,3,2,1,0:T(8,128)(2,1)}, u32[]{:S(2)}) %copy-start.1) | copy-done | bytes 524312
  3.6 0.0 copy-start.2
  3.6 0.9 %copy-done.2 = f32[1,256,256]{2,1,0:T(8,128)S(1)} copy-done((f32[1,256,256]{2,1,0:T(8,128)S(1)}, f32[1,256,256]{2,1,0:T(8,128)}, u32[]{:S(2)}) %copy-start.2) | copy-done | bytes 262168
  4.5 25.0 %shard_map.77 = (f32[4,256,256]{2,1,0:T(8,128)S(1)}, bf16[4,256,256]{2,1,0:T(8,128)(2,1)S(1)}) custom-call(f32[4,256,256]{2,1,0:T(8,128)S(1)} %bitcast.7, f32[256,256]{1,0:T(8,128)S(1)} %bitcast.11, bf16[2,2,256,256]{3,2,1,0:T(8,128)(2,1)S(1)} %bitcast.9, s32[2,2]{1,0:T(2,128)S(1)} %bitcast.12, s32[2]{0:T(128)S(1)} %bitcast.13, s32[2,16]{1,0:T(2,128)S(1)} %copy-done.4), custom_call_target="tpu_custom_call" | custom-call | flops 402653184 | bytes 2097152 | tf_op jit(solution)/shard_map/pallas_call | solution.py:205
  29.5 1.0 %copy.10 = f32[1,1024,256]{2,1,0:T(8,128)} copy(f32[1,1024,256]{2,1,0:T(8,128)S(1)} %bitcast.8) | data formatting | bytes 2097152
  30.5 0.8 %copy.11 = bf16[1,1,4,256,256]{4,3,2,1,0:T(8,128)(2,1)} copy(bf16[1,1,4,256,256]{4,3,2,1,0:T(8,128)(2,1)S(1)} %bitcast.10) | data formatting | bytes 1048576
Async XLA Ops:
  0.6 0.7 %copy-start.4 = (s32[2,16]{1,0:T(2,128)S(1)}, s32[2,16]{1,0:T(2,128)}, u32[]{:S(2)}) copy-start(s32[2,16]{1,0:T(2,128)} %plan.1) | copy-start | bytes 388
  0.6 0.7 %copy-start.3 = (s32[1,1,2,2]{3,2,1,0:T(2,128)S(1)}, s32[1,1,2,2]{3,2,1,0:T(2,128)}, u32[]{:S(2)}) copy-start(s32[1,1,2,2]{3,2,1,0:T(2,128)} %param.9) | copy-start | bytes 52
  0.7 0.7 %copy-start.5 = (s32[1,1,2]{2,1,0:T(1,128)S(1)}, s32[1,1,2]{2,1,0:T(1,128)}, u32[]{:S(2)}) copy-start(s32[1,1,2]{2,1,0:T(1,128)} %param.10) | copy-start | bytes 28
  1.3 1.2 %copy-start = (f32[1,1024,256]{2,1,0:T(8,128)S(1)}, f32[1,1024,256]{2,1,0:T(8,128)}, u32[]{:S(2)}) copy-start(f32[1,1024,256]{2,1,0:T(8,128)} %param.6) | copy-start | bytes 3145732
  2.6 1.0 %copy-start.1 = (bf16[1,1,2,2,256,256]{5,4,3,2,1,0:T(8,128)(2,1)S(1)}, bf16[1,1,2,2,256,256]{5,4,3,2,1,0:T(8,128)(2,1)}, u32[]{:S(2)}) copy-start(bf16[1,1,2,2,256,256]{5,4,3,2,1,0:T(8,128)(2,1)} %param.8) | copy-start | bytes 1572868
  3.6 0.9 %copy-start.2 = (f32[1,256,256]{2,1,0:T(8,128)S(1)}, f32[1,256,256]{2,1,0:T(8,128)}, u32[]{:S(2)}) copy-start(f32[1,256,256]{2,1,0:T(8,128)} %param.7) | copy-start | bytes 786436

commit v2 on v1

v2 whole, which is shorter than its diff:
```python
import functools

import jax
import jax.numpy as jnp
from jax import lax
from jax.experimental import pallas as pl
from jax.experimental.pallas import tpu as pltpu
from jax.sharding import PartitionSpec as P

CAP = 4
PARTS = 2
CHUNKS = 2
VMEM_GRANT = 63 * 1024 * 1024

learn_rate = 0.01
shrinkage = 0.05

MESH = pl.DeviceIdType.MESH
F32 = jnp.float32
LOW = jnp.bfloat16


def kernel(
    blocks, groups, parts, chunks,
    users_hbm, items_hbm, ratings_hbm, row_table, count_table, plan,
    users_out, received,
    users, items, ratings, ring_out, ring_in, handed, staged, change, picks,
    load_sem, ring_send, ring_recv, part_send, part_recv, slot_send, slot_recv, own_sem, out_sem,
    *gathered,
):
    stops, capt = ratings.shape[0], ratings.shape[1]
    tiles = users.shape[0]
    lanes = blocks // parts
    depth = gathered[0].shape[1]
    width = depth * lanes
    me = lax.axis_index("blk")
    group = lax.axis_index("group")
    ahead, behind = lax.rem(group + 1, groups), lax.rem(group + groups - 1, groups)
    right, left = lax.rem(me + 1, blocks), lax.rem(me + blocks - 1, blocks)
    part_first = (me // lanes) * lanes
    lane = me - part_first

    loads = [pltpu.make_async_copy(items_hbm, items, load_sem.at[0])]
    loads.append(pltpu.make_async_copy(users_hbm, users, load_sem.at[1]))
    for stop in range(stops):
        loads.append(
            pltpu.make_async_copy(ratings_hbm.at[stop], ratings.at[stop], load_sem.at[2 + stop])
        )
    for load in loads:
        load.start()

    barrier = pltpu.get_barrier_semaphore()
    pl.semaphore_signal(barrier, inc=1, device_id=(left, group), device_id_type=MESH)
    for step in range(blocks):
        pl.semaphore_signal(
            barrier, inc=1, device_id=(lax.rem(me + step, blocks), behind), device_id_type=MESH
        )
    for step in range(1, lanes):
        other = part_first + lax.rem(lane + step, lanes)
        pl.semaphore_signal(barrier, inc=1, device_id=(other, group), device_id_type=MESH)

    change[capt] = jnp.zeros(change.shape[1:], F32)
    for chunk in range(chunks):
        gathered[chunk][blocks] = jnp.zeros(gathered[chunk].shape[1:], LOW)

    def ring_copy(stop, chunk, half):
        return pltpu.make_async_remote_copy(
            src_ref=ring_out.at[stop, chunk, half],
            dst_ref=ring_in.at[stop, chunk, half],
            send_sem=ring_send.at[stop, chunk, half],
            recv_sem=ring_recv.at[stop, chunk, half],
            device_id=(right, group),
            device_id_type=MESH,
        )

    def part_copy(chunk, step):
        target = lax.rem(me + step, blocks)
        first = pl.multiple_of(lax.rem(target, lanes) * depth, depth)
        return pltpu.make_async_remote_copy(
            src_ref=handed.at[chunk, pl.ds(first, depth)],
            dst_ref=gathered[chunk].at[me],
            send_sem=part_send.at[chunk, step],
            recv_sem=part_recv.at[chunk, me],
            device_id=(target, ahead),
            device_id_type=MESH,
        )

    def slot_rows(chunk, holder):
        return pl.ds(pl.multiple_of(chunk * width + holder * depth, depth), depth)

    def slot_copy(chunk, step):
        return pltpu.make_async_remote_copy(
            src_ref=staged.at[chunk, step],
            dst_ref=received.at[:, slot_rows(chunk, lane)],
            send_sem=slot_send.at[chunk, step],
            recv_sem=slot_recv.at[chunk, lane],
            device_id=(part_first + lax.rem(lane + step, lanes), group),
            device_id_type=MESH,
        )

    loads[0].wait()
    loads[1].wait()
    for stop in range(stops):
        loads[2 + stop].wait()
        count = count_table[stop]
        active = [(c < count).astype(F32) for c in range(capt)]
        user_low = [users[row_table[stop, c]].astype(LOW) for c in range(capt)]
        kept = []
        for chunk in range(chunks):
            rows = slice(chunk * width, (chunk + 1) * width)
            if stop == 0:
                item_low = items[rows].astype(LOW)
            else:
                ring_copy(stop - 1, chunk, 0).wait_recv()
                item_low = ring_in[stop - 1, chunk, 0]
            grad = jnp.zeros((width, items.shape[1]), F32)
            residuals = []
            for c in range(capt):
                predicted = lax.dot_general(
                    user_low[c], item_low, (((1,), (1,)), ((), ())), preferred_element_type=F32
                )
                residual = (
                    active[c] * (ratings[stop, c, :, rows].astype(F32) - predicted)
                ).astype(LOW)
                grad = grad + lax.dot_general(
                    residual, user_low[c], (((0,), (0,)), ((), ())), preferred_element_type=F32
                )
                residuals.append(residual)
            kept.append((item_low, residuals))
            if stop == 0:
                block = items[rows]
            else:
                ring_copy(stop - 1, chunk, 1).wait_recv()
                block = item_low.astype(F32) + ring_in[stop - 1, chunk, 1].astype(F32)
            block = block + learn_rate * (grad - shrinkage * count.astype(F32) * block)
            if stop == 0 and chunk == 0:
                pl.semaphore_wait(barrier, blocks + lanes)
            if stop < stops - 1:
                high = block.astype(LOW)
                ring_out[stop, chunk, 0] = high
                ring_copy(stop, chunk, 0).start()
                ring_out[stop, chunk, 1] = (block - high.astype(F32)).astype(LOW)
                ring_copy(stop, chunk, 1).start()
            else:
                handed[chunk] = block.astype(LOW)
                for step in range(blocks):
                    part_copy(chunk, step).start()
        for c in range(capt):
            before = users[row_table[stop, c]]
            user_step = jnp.zeros(before.shape, F32)
            for item_low, residuals in kept:
                user_step = user_step + jnp.dot(
                    residuals[c], item_low, preferred_element_type=F32
                )
            change[c] = learn_rate * active[c] * (user_step - shrinkage * before)
        for tile in range(tiles):
            which = jnp.int32(capt)
            for c in range(capt):
                which = jnp.where(row_table[stop, c] == tile, c, which)
            users[tile] = users[tile] + change[which]
    save = pltpu.make_async_copy(users, users_out, out_sem)
    save.start()

    def find(step, carry):
        target = part_first + lax.rem(lane + step, lanes)
        seen = jnp.int32(0)
        found = [jnp.int32(blocks)] * CAP
        for k in range(blocks):
            match = plan[behind, k] == target
            for c in range(CAP):
                found[c] = jnp.where(match & (seen == c), (k + stops - 1) % blocks, found[c])
            seen = seen + match.astype(jnp.int32)
        for c in range(CAP):
            picks[step, c] = found[c]
        return carry

    lax.fori_loop(0, lanes, find, 0)

    own = []
    for chunk in range(chunks):
        for k in range(blocks):
            pltpu.make_async_remote_copy(
                src_ref=gathered[chunk].at[k],
                dst_ref=gathered[chunk].at[k],
                send_sem=part_send.at[chunk, k],
                recv_sem=part_recv.at[chunk, k],
                device_id=(k, behind),
                device_id_type=MESH,
            ).wait_recv()
        for step in list(range(1, lanes)) + [0]:
            for c in range(CAP):
                staged[chunk, step, c] = gathered[chunk][picks[step, c]]
            if step > 0:
                slot_copy(chunk, step).start()
        own.append(
            pltpu.make_async_copy(
                staged.at[chunk, 0], received.at[:, slot_rows(chunk, lane)], own_sem.at[chunk]
            )
        )
        own[-1].start()
    for chunk in range(chunks):
        for step in range(1, lanes):
            sender = lax.rem(lane + step, lanes)
            pltpu.make_async_remote_copy(
                src_ref=staged.at[chunk, step],
                dst_ref=received.at[:, slot_rows(chunk, sender)],
                send_sem=slot_send.at[chunk, step],
                recv_sem=slot_recv.at[chunk, sender],
                device_id=(part_first + sender, group),
                device_id_type=MESH,
            ).wait_recv()
    for chunk in range(chunks):
        own[chunk].wait()
        for step in range(1, lanes):
            slot_copy(chunk, step).wait_send()
        for step in range(blocks):
            part_copy(chunk, step).wait_send()
        for stop in range(stops - 1):
            for half in range(2):
                ring_copy(stop, chunk, half).wait_send()
    save.wait()


def shards(user_factors, item_factors, ratings, tile_rows, counts, plan):
    blocks, groups = lax.axis_size("blk"), lax.axis_size("group")
    _, _, stops, capt, tile, _ = ratings.shape
    _, rows, rank = user_factors.shape
    item_rows = item_factors.shape[1]
    parts = max(PARTS, blocks * 16 // item_rows)
    lanes = blocks // parts
    chunks = max(1, min(CHUNKS, item_rows // (lanes * 16)))
    width = item_rows // chunks
    depth = width // lanes
    tiled = (rows // tile, tile, rank)
    hbm = pl.BlockSpec(memory_space=pltpu.HBM)
    smem = pl.BlockSpec(memory_space=pltpu.SMEM)
    place = pl.BlockSpec(memory_space=pl.ANY)
    hops = max(stops - 1, 1)
    users, received = pl.pallas_call(
        functools.partial(kernel, blocks, groups, parts, chunks),
        out_shape=(
            jax.ShapeDtypeStruct(tiled, F32),
            jax.ShapeDtypeStruct((CAP, item_rows, rank), LOW),
        ),
        in_specs=[hbm, hbm, hbm, smem, smem, smem],
        out_specs=(place, place),
        scratch_shapes=[
            pltpu.VMEM(tiled, F32),
            pltpu.VMEM((item_rows, rank), F32),
            pltpu.VMEM(ratings.shape[2:], LOW),
            pltpu.VMEM((hops, chunks, 2, width, rank), LOW),
            pltpu.VMEM((hops, chunks, 2, width, rank), LOW),
            pltpu.VMEM((chunks, width, rank), LOW),
            pltpu.VMEM((chunks, lanes, CAP, depth, rank), LOW),
            pltpu.VMEM((capt + 1, tile, rank), F32),
            pltpu.SMEM((lanes, CAP), jnp.int32),
            pltpu.SemaphoreType.DMA((2 + stops,)),
            pltpu.SemaphoreType.DMA((hops, chunks, 2)),
            pltpu.SemaphoreType.DMA((hops, chunks, 2)),
            pltpu.SemaphoreType.DMA((chunks, blocks)),
            pltpu.SemaphoreType.DMA((chunks, blocks)),
            pltpu.SemaphoreType.DMA((chunks, lanes)),
            pltpu.SemaphoreType.DMA((chunks, lanes)),
            pltpu.SemaphoreType.DMA((chunks,)),
            pltpu.SemaphoreType.DMA,
        ]
        + [pltpu.VMEM((blocks + 1, depth, rank), LOW)] * chunks,
        compiler_params=pltpu.CompilerParams(
            collective_id=0, has_side_effects=True, vmem_limit_bytes=VMEM_GRANT
        ),
        cost_estimate=pl.CostEstimate(
            flops=6 * stops * capt * tile * item_rows * rank,
            bytes_accessed=2 * rows * rank * 4,
            transcendentals=0,
        ),
    )(
        user_factors.reshape(tiled),
        item_factors[0],
        ratings[0, 0],
        tile_rows[0, 0],
        counts[0, 0],
        plan,
    )
    return users.reshape(1, rows, rank), received[None, None]


def solution(mesh):
    in_specs = (
        P("group", "blk", None),
        P("group", "blk", None),
        P("group", "blk", None, None, None, None),
        P("group", "blk", None, None),
        P("group", "blk", None),
        P(),
    )
    out_specs = (P("group", "blk", None), P("group", "blk", None, None, None))
    return jax.shard_map(shards, mesh=mesh, in_specs=in_specs, out_specs=out_specs, check_vma=False)
```

time: 31.8 us -> 28.7 us (0.903); the launches traced: 31.3 us -> 28.6 us
  local copies, waits for them, and re-layouts: 5.65 us -> 3.12 us
    unnamed x14 -> x4, local copies, waits for them, and re-layouts: 5.65 us -> 3.12 us
where the time goes in v2:
time: 28.7 us; the launch traced here: 28.6 us
  Pallas kernels  24.8 us (86%)
  local copies, waits for them, and re-layouts  3.12 us (11%)
  between operations  0.65 us (2%)
    pallas_call x1, Pallas kernels, shards(): pl.pallas_call(functools.partial(kernel, blocks, groups, parts, chunks),...  24.8 us
    unnamed x4, local copies, waits for them, and re-layouts  3.12 us

profile of v2, /device:TPU:0, one launch (start us, length us, event | category | flops | bytes accessed | tf_op | source)
XLA Modules:
  0.0 28.6 jit_solution(5267800555220264441)
XLA Ops:
  0.6 24.8 %shard_map.77 = (f32[4,256,256]{2,1,0:T(8,128)}, bf16[4,256,256]{2,1,0:T(8,128)(2,1)}) custom-call(f32[4,256,256]{2,1,0:T(8,128)} %bitcast.7, f32[256,256]{1,0:T(8,128)} %bitcast.11, bf16[2,2,256,256]{3,2,1,0:T(8,128)(2,1)} %bitcast.9, s32[2,2]{1,0:T(2,128)} %bitcast.12, s32[2]{0:T(128)} %bitcast.13, s32[2,16]{1,0:T(2,128)} %plan.1), custom_call_target="tpu_custom_call" | custom-call | flops 402653184 | bytes 2097152 | tf_op jit(solution)/shard_map/pallas_call | solution.py:239
  25.4 0.0 copy-start
  25.4 2.3 %copy.10 = f32[1,1024,256]{2,1,0:T(8,128)} copy(f32[1,1024,256]{2,1,0:T(8,128)} %bitcast.8) | data formatting | bytes 2097152
  27.8 0.0 copy-done
  27.8 0.8 %copy.11 = bf16[1,1,4,256,256]{4,3,2,1,0:T(8,128)(2,1)} copy(bf16[1,1,4,256,256]{4,3,2,1,0:T(8,128)(2,1)S(1)} %bitcast.10) | data formatting | bytes 1048576
Async XLA Ops:
  25.4 2.3 %copy-start = (bf16[4,256,256]{2,1,0:T(8,128)(2,1)S(1)}, bf16[4,256,256]{2,1,0:T(8,128)(2,1)}, u32[]{:S(2)}) copy-start(bf16[4,256,256]{2,1,0:T(8,128)(2,1)} %get-tuple-element.5) | copy-start | bytes 1572868

commit v3 on v2

--- a/solution.py
+++ b/solution.py
@@ -221,6 +221,21 @@
     save.wait()
 
 
+def deliver(users, received, users_out, received_out, sem):
+    tiles, slots = users.shape[0], received.shape[0]
+    copies = [
+        pltpu.make_async_copy(users.at[t], users_out.at[t], sem.at[t]) for t in range(tiles)
+    ]
+    for c in range(slots):
+        copies.append(
+            pltpu.make_async_copy(received.at[c], received_out.at[c], sem.at[tiles + c])
+        )
+    for copy in copies:
+        copy.start()
+    for copy in copies:
+        copy.wait()
+
+
 def shards(user_factors, item_factors, ratings, tile_rows, counts, plan):
     blocks, groups = lax.axis_size("blk"), lax.axis_size("group")
     _, _, stops, capt, tile, _ = ratings.shape
@@ -281,6 +296,17 @@
         counts[0, 0],
         plan,
     )
+    users, received = pl.pallas_call(
+        deliver,
+        out_shape=(
+            jax.ShapeDtypeStruct(tiled, F32),
+            jax.ShapeDtypeStruct((CAP, item_rows, rank), LOW),
+        ),
+        in_specs=[place, place],
+        out_specs=(hbm, hbm),
+        scratch_shapes=[pltpu.SemaphoreType.DMA((tiled[0] + CAP,))],
+        compiler_params=pltpu.CompilerParams(has_side_effects=True),
+    )(users, received)
     return users.reshape(1, rows, rank), received[None, None]
 
 

time: 28.7 us -> 74.4 us (2.59)
  Pallas kernels: 24.8 us -> 73.6 us
  local copies, waits for them, and re-layouts: 3.12 us -> 0 us
    pallas_call x0 -> x1, Pallas kernels: none -> 48.8 us  [shards(): pl.pallas_call(deliver, out_shape=(jax.ShapeDtypeStruct(tiled, F32), jax....]
    unnamed x4 -> x0, local copies, waits for them, and re-layouts: 3.12 us -> none
where the time goes in v3:
time: 74.4 us; the launch traced here: 74.2 us
  Pallas kernels  73.6 us (99%)
    pallas_call x1, Pallas kernels, shards(): pl.pallas_call(deliver, out_shape=(jax.ShapeDtypeStruct(tiled, F32), jax....  48.8 us
    pallas_call x1, Pallas kernels, shards(): pl.pallas_call(functools.partial(kernel, blocks, groups, parts, chunks),...  24.8 us

profile of v3, /device:TPU:0, one launch (start us, length us, event | category | flops | bytes accessed | tf_op | source)
XLA Modules:
  0.0 74.2 jit_solution(885399865253049864)
XLA Ops:
  0.6 24.8 %shard_map.77 = (f32[4,256,256]{2,1,0:T(8,128)}, bf16[4,256,256]{2,1,0:T(8,128)(2,1)}) custom-call(f32[4,256,256]{2,1,0:T(8,128)} %bitcast.7, f32[256,256]{1,0:T(8,128)} %bitcast.9, bf16[2,2,256,256]{3,2,1,0:T(8,128)(2,1)} %bitcast.8, s32[2,2]{1,0:T(2,128)} %bitcast.10, s32[2]{0:T(128)} %bitcast.11, s32[2,16]{1,0:T(2,128)} %plan.1), custom_call_target="tpu_custom_call" | custom-call | flops 402653184 | bytes 2097152 | tf_op jit(solution)/shard_map/pallas_call | solution.py:254
  25.4 48.8 %shard_map.78 = (f32[4,256,256]{2,1,0:T(8,128)}, bf16[4,256,256]{2,1,0:T(8,128)(2,1)}) custom-call(f32[4,256,256]{2,1,0:T(8,128)} %get-tuple-element.6.users, bf16[4,256,256]{2,1,0:T(8,128)(2,1)} %get-tuple-element.7.received), custom_call_target="tpu_custom_call" | custom-call | tf_op jit(solution)/shard_map/pallas_call | solution.py:299

commit v4 on v3

--- a/solution.py
+++ b/solution.py
@@ -221,18 +221,20 @@
     save.wait()
 
 
-def deliver(users, received, users_out, received_out, sem):
+def deliver(users, received, users_out, received_out, users_held, slots_held, in_sem, out_sem):
     tiles, slots = users.shape[0], received.shape[0]
-    copies = [
-        pltpu.make_async_copy(users.at[t], users_out.at[t], sem.at[t]) for t in range(tiles)
-    ]
-    for c in range(slots):
-        copies.append(
-            pltpu.make_async_copy(received.at[c], received_out.at[c], sem.at[tiles + c])
-        )
-    for copy in copies:
+    moves = [(users, users_held, users_out, t) for t in range(tiles)]
+    moves += [(received, slots_held, received_out, c) for c in range(slots)]
+    ins, outs = [], []
+    for i, (source, held, target, at) in enumerate(moves):
+        ins.append(pltpu.make_async_copy(source.at[at], held.at[at], in_sem.at[i]))
+        outs.append(pltpu.make_async_copy(held.at[at], target.at[at], out_sem.at[i]))
+    for copy in ins:
         copy.start()
-    for copy in copies:
+    for copy_in, copy_out in zip(ins, outs):
+        copy_in.wait()
+        copy_out.start()
+    for copy in outs:
         copy.wait()
 
 
@@ -304,8 +306,13 @@
         ),
         in_specs=[place, place],
         out_specs=(hbm, hbm),
-        scratch_shapes=[pltpu.SemaphoreType.DMA((tiled[0] + CAP,))],
-        compiler_params=pltpu.CompilerParams(has_side_effects=True),
+        scratch_shapes=[
+            pltpu.VMEM(tiled, F32),
+            pltpu.VMEM((CAP, item_rows, rank), LOW),
+            pltpu.SemaphoreType.DMA((tiled[0] + CAP,)),
+            pltpu.SemaphoreType.DMA((tiled[0] + CAP,)),
+        ],
+        compiler_params=pltpu.CompilerParams(vmem_limit_bytes=VMEM_GRANT),
     )(users, received)
     return users.reshape(1, rows, rank), received[None, None]
 

time: 74.4 us -> 27.8 us (0.37)
  Pallas kernels: 73.6 us -> 27 us
    pallas_call x1, Pallas kernels: 48.8 us -> 2.22 us  [shards(): pl.pallas_call(deliver, out_shape=(jax.ShapeDtypeStruct(tiled, F32), jax....]
where the time goes in v4:
time: 27.8 us; the launch traced here: 27.6 us
  Pallas kernels  27 us (97%)
  between operations  0.64 us (2%)
    pallas_call x1, Pallas kernels, shards(): pl.pallas_call(functools.partial(kernel, blocks, groups, parts, chunks),...  24.8 us
    pallas_call x1, Pallas kernels, shards(): pl.pallas_call(deliver, out_shape=(jax.ShapeDtypeStruct(tiled, F32), jax....  2.22 us

profile of v4, /device:TPU:0, one launch (start us, length us, event | category | flops | bytes accessed | tf_op | source)
XLA Modules:
  0.0 27.6 jit_solution(11919870088841858081)
XLA Ops:
  0.6 24.8 %shard_map.77 = (f32[4,256,256]{2,1,0:T(8,128)}, bf16[4,256,256]{2,1,0:T(8,128)(2,1)}) custom-call(f32[4,256,256]{2,1,0:T(8,128)} %bitcast.7, f32[256,256]{1,0:T(8,128)} %bitcast.9, bf16[2,2,256,256]{3,2,1,0:T(8,128)(2,1)} %bitcast.8, s32[2,2]{1,0:T(2,128)} %bitcast.10, s32[2]{0:T(128)} %bitcast.11, s32[2,16]{1,0:T(2,128)} %plan.1), custom_call_target="tpu_custom_call" | custom-call | flops 402653184 | bytes 2097152 | tf_op jit(solution)/shard_map/pallas_call | solution.py:256
  25.4 2.2 %shard_map.78 = (f32[4,256,256]{2,1,0:T(8,128)}, bf16[4,256,256]{2,1,0:T(8,128)(2,1)}) custom-call(f32[4,256,256]{2,1,0:T(8,128)} %get-tuple-element.6.users, bf16[4,256,256]{2,1,0:T(8,128)(2,1)} %get-tuple-element.7.received), custom_call_target="tpu_custom_call" | custom-call | tf_op jit(solution)/shard_map/pallas_call | solution.py:301
